TPU v7x, 256 devices: a whole 4x4x8 slice. The times are simulated.
256 devices in a mesh: ctx: 16 (over x, z_lo, core), exp: 16 (over y, z_hi).
Axes of the slice: x: 4, y: 4, z: 8 (z_hi: 4, z_lo: 2; z = z_hi * 2 + z_lo), core: 2. Of those that a mesh axis runs over, the one named last changes fastest.
Arguments:
- queries: bfloat16 [2048, 64, 192], P('ctx', 'exp'), may hold values from -8 to 8
- latent_cache: bfloat16 [4096, 576], P('ctx'), may hold values from -8 to 8
- group_latent: bfloat16 [2048, 576], P('ctx'), may hold values from -6 to 6
- w_absorb_k: bfloat16 [64, 128, 512], P('exp'), may hold values from -0.5 to 0.5
- value_absorb_weight: bfloat16 [64, 512, 128], P('exp'), may hold values from -1 to 1
- w_out: bfloat16 [8192, 7168], P('exp', 'ctx'), may hold values from -0.1875 to 0.1875
- residual: bfloat16 [2048, 7168], P('exp', 'ctx'), may hold values from -12 to 12
- norm_gain: float32 [7168], P('ctx'), may hold values from 0.5 to 1.5
- routes: int32 [2048, 1], P('exp'), may hold values from 0 to 15; in each aligned block of 128 rows (0 to 127, 128 to 255, ...) at most 16 rows name the same one
- route_weight: float32 [2048, 1], P('exp'), may hold values from 0.3 to 3
- w_gate: bfloat16 [16, 7168, 2048], P('exp', 'ctx'), may hold values from -0.0625 to 0.0625
- w_up: bfloat16 [16, 7168, 2048], P('exp', 'ctx'), may hold values from -0.0625 to 0.0625
- w_down: bfloat16 [16, 2048, 7168], P('exp', None, 'ctx'), may hold values from -0.125 to 0.125
Outputs:
- mixed: bfloat16 [2048, 7168], P('exp', 'ctx')
Inputs may be any that keep to these rules, and one draw needn't show every extreme that they name: `routes`: in each aligned block of 128 rows (the rows of one exp index), no expert is named by more than 16 rows, a bound that some block reaches.
All inputs are finite; a program needn't handle non-finite values.
Results may differ from a plain program's by a relative error of at most 0.022.
Values may be sent and summed in bfloat16 or wider, within the bound.
A program may use at most 64 MiB of HBM per device.

v0:
```python
import math

import jax
import jax.numpy as jnp
from jax import lax
from jax.sharding import PartitionSpec as P

D = 7168
TOP = 1
CAP = 16


def per_device(
    queries,
    latent_cache,
    group_latent,
    w_absorb_k,
    value_absorb_weight,
    w_out,
    residual,
    norm_gain,
    routes,
    route_weight,
    w_gate,
    w_up,
    w_down,
):
    token_count, head_count, query_width = queries.shape
    nope_width = w_absorb_k.shape[1]
    rank = w_absorb_k.shape[2]
    key_width = rank + query_width - nope_width
    lowered = jnp.einsum(
        "thn,hnk->thk", queries[:, :, :nope_width], w_absorb_k, preferred_element_type=jnp.float32
    ).astype(jnp.bfloat16)
    absorbed_query = jnp.concatenate([lowered, queries[:, :, nope_width:]], axis=2).reshape(
        token_count * head_count, key_width
    )
    row_total = token_count * head_count
    inverse_scale = 1.0 / math.sqrt(query_width)
    query_index = lax.axis_index("ctx") * token_count + jnp.arange(row_total) // head_count
    initial = (
        jnp.full((row_total,), -1e30, jnp.float32),
        jnp.zeros((row_total,), jnp.float32),
        jnp.zeros((row_total, rank), jnp.float32),
    )

    def fold_keys(running, piece, visible):
        peak, total, numerator = running
        scores = (
            lax.dot_general(
                absorbed_query, piece, (((1,), (1,)), ((), ())), preferred_element_type=jnp.float32
            )
            * inverse_scale
        )
        masked = jnp.where(visible, scores, -1e30)
        new_peak = jnp.maximum(peak, jnp.max(masked, axis=1))
        weights = jnp.where(visible, jnp.exp(masked - new_peak[:, None]), 0.0)
        decay = jnp.exp(peak - new_peak)
        total = total * decay + jnp.sum(weights, axis=1)
        numerator = numerator * decay[:, None] + jnp.dot(
            weights.astype(jnp.bfloat16), piece[:, :rank], preferred_element_type=jnp.float32
        )
        return (new_peak, total, numerator)

    running = fold_keys(
        initial,
        lax.all_gather(latent_cache, "ctx", axis=0, tiled=True),
        jnp.ones((1, 1), jnp.bool_),
    )
    piece = lax.all_gather(group_latent, "ctx", axis=0, tiled=True)
    key_index = jnp.arange(piece.shape[0])
    running = fold_keys(running, piece, key_index[None, :] <= query_index[:, None])
    context_vector = (
        (running[2] / running[1][:, None])
        .astype(jnp.bfloat16)
        .reshape(token_count, head_count, rank)
    )
    per_head_output = jnp.einsum(
        "qbc,bcg->qbg", context_vector, value_absorb_weight, preferred_element_type=jnp.float32
    ).astype(jnp.bfloat16)
    per_head_output = per_head_output.reshape(
        token_count, head_count * value_absorb_weight.shape[2]
    )
    gathered = lax.all_gather(per_head_output, "ctx", axis=0, tiled=True)
    attended = lax.psum_scatter(
        jnp.dot(gathered, w_out, preferred_element_type=jnp.float32).astype(jnp.bfloat16),
        "exp",
        scatter_dimension=0,
        tiled=True,
    ).astype(jnp.float32)
    state = residual.astype(jnp.float32) + attended
    square_sums = lax.psum(jnp.sum(state * state, axis=1), "ctx")
    normed = (state * lax.rsqrt(square_sums / D + 1e-06)[:, None] * norm_gain[None, :]).astype(
        jnp.bfloat16
    )
    expert_count = lax.axis_size("exp")
    route_row = routes.reshape(-1)
    onehot = (route_row[:, None] == jnp.arange(expert_count)[None, :]).astype(jnp.int32)
    earlier = jnp.cumsum(onehot, axis=0) - onehot
    slot = jnp.sum(earlier * onehot, axis=1)
    target = route_row * CAP + slot
    slot_lookup_table = (jnp.arange(expert_count * CAP)[:, None] == target[None, :]).astype(
        jnp.bfloat16
    )
    pairs = jnp.repeat(normed, TOP, axis=0)
    width = normed.shape[1]
    outgoing = (
        jnp.dot(slot_lookup_table, pairs, preferred_element_type=jnp.float32)
        .astype(jnp.bfloat16)
        .reshape(expert_count, CAP, width)
    )
    received = lax.all_to_all(outgoing, "exp", split_axis=0, concat_axis=0, tiled=True)
    sources, slots, _ = received.shape
    expert_rows = received.reshape(sources * slots, width)
    gate = jnp.dot(expert_rows, w_gate[0], preferred_element_type=jnp.float32)
    up = jnp.dot(expert_rows, w_up[0], preferred_element_type=jnp.float32)
    stacked = jnp.stack((gate, up), axis=1)
    summed = lax.psum(stacked.astype(jnp.bfloat16), "ctx").astype(jnp.float32)
    hidden = (jax.nn.silu(summed[:, 0]) * summed[:, 1]).astype(jnp.bfloat16)
    expert_out = jnp.dot(hidden, w_down[0], preferred_element_type=jnp.float32).astype(jnp.bfloat16)
    returned = lax.all_to_all(
        expert_out.reshape(sources, slots, width), "exp", split_axis=0, concat_axis=0, tiled=True
    )
    flattened = returned.reshape(expert_count * CAP, width)
    token_out = lax.dot_general(
        slot_lookup_table, flattened, (((0,), (0,)), ((), ())), preferred_element_type=jnp.float32
    )
    token_out = token_out.reshape(routes.shape[0], TOP, width)
    routed = jnp.sum(token_out * route_weight[:, :, None], axis=1)
    return (state + routed).astype(jnp.bfloat16)


def solution(mesh):
    in_specs = (
        P("ctx", "exp", None),
        P("ctx", None),
        P("ctx", None),
        P("exp", None, None),
        P("exp", None, None),
        P("exp", "ctx"),
        P("exp", "ctx"),
        P("ctx"),
        P("exp", None),
        P("exp", None),
        P("exp", "ctx", None),
        P("exp", "ctx", None),
        P("exp", None, "ctx"),
    )
    out_specs = P("exp", "ctx")
    return jax.shard_map(
        per_device, mesh=mesh, in_specs=in_specs, out_specs=out_specs, check_vma=False
    )
```

profile of v0, /device:TPU:1, one launch (start us, length us, event | category | flops | bytes accessed | tf_op | source)
XLA Modules:
  0.0 458.0 jit_solution(15730595423020734170)
XLA Ops:
  6.5 0.0 copy-start
  6.5 0.0 all-gather.6.cloned.1.call-start
  6.5 0.7 all-gather.6.cloned.1.call-update
  7.3 0.0 all-gather.4.cloned.1.call-start
  7.3 0.7 all-gather.4.cloned.1.call-update
  8.0 0.0 all-gather.8.cloned.1.call-start
  8.1 0.9 slice.19
  8.9 1.4 fusion.39
  10.4 0.8 copy.27
  11.2 0.3 reshape.86
  11.5 42.6 %all-gather.6.cloned.1.call-done = bf16[2048,576]{0,1:T(8,128)(2,1)} async-done(((bf16[128,576]{0,1:T(8,128)(2,1)}), bf16[2048,576]{0,1:T(8,128)(2,1)}) %all-gather.6.cloned.1.call-update) | async-done | bytes 2359312 | tf_op jit(solution)/shard_map/all_gather | solution.py:70
  54.1 5.7 %fusion.7 = (f32[512]{0:T(512)S(1)}, f32[512,2048]{1,0:T(8,128)}) fusion(s32[512]{0:T(512)S(1)} %fusion.58, bf16[512,576]{1,0:T(8,128)(2,1)S(1)} %reshape.86, bf16[2048,576]{0,1:T(8,128)(2,1)} %all-gather.6.cloned.1.call-done), kind=kOutput, calls=%fused_computation.11 | convolution fusion | flops 1212153344 | bytes 7147520 | tf_op jit(solution)/shard_map/dot_general | solution.py:50
  59.8 47.3 %all-gather.4.cloned.1.call-done = bf16[4096,576]{0,1:T(8,128)(2,1)} async-done(((bf16[256,576]{0,1:T(8,128)(2,1)}), bf16[4096,576]{0,1:T(8,128)(2,1)}) %all-gather.4.cloned.1.call-update) | async-done | bytes 4718608 | tf_op jit(solution)/shard_map/all_gather | solution.py:67
  107.1 0.0 copy-start.1
  107.1 5.6 %multiply_reduce_fusion = (f32[512]{0:T(512)S(1)}, f32[512,4096]{1,0:T(8,128)S(1)}) fusion(bf16[512,576]{1,0:T(8,128)(2,1)S(1)} %reshape.86, bf16[4096,576]{0,1:T(8,128)(2,1)} %all-gather.4.cloned.1.call-done), kind=kOutput, calls=%fused_computation.1 | convolution fusion | flops 2420112896 | bytes 13699072 | tf_op jit(solution)/shard_map/dot_general | solution.py:50
  112.8 0.0 copy-done.1
  112.8 0.0 slice-start
  112.8 1.4 fusion.10
  114.2 0.0 slice-start.1
  114.2 1.5 fusion
  115.7 0.0 slice-done
  115.7 0.0 slice-done.1
  115.7 0.0 copy-start.7
  115.7 2.4 fusion.34
  118.2 0.0 copy-done.7
  118.2 0.0 copy-start.3
  118.2 1.6 divide_convert_fusion
  119.7 0.1 reshape.87
  119.9 0.0 copy-done.3
  119.9 1.0 convolution_convert_fusion.5
  120.9 0.0 all-gather.8.cloned.1.call-update
  120.9 0.2 reduce-scatter.4.cloned.1.call-start
  121.2 38.5 %all-gather.8.cloned.1.call-done = bf16[2048,512]{0,1:T(8,128)(2,1)} async-done(((bf16[128,512]{0,1:T(8,128)(2,1)}), bf16[2048,512]{0,1:T(8,128)(2,1)}) %all-gather.8.cloned.1.call-update) | async-done | bytes 2097168 | tf_op jit(solution)/shard_map/all_gather | solution.py:84
  159.7 4.1 convolution_convert_fusion
  163.8 3.9 copy.34
  167.6 0.0 reduce-scatter.4.cloned.1.call-update
  167.7 0.0 all-reduce.2.cloned.1.call-start
  167.7 0.0 copy-done.5
  167.7 0.1 fusion.57
  167.8 0.2 reduce_window_sum.11
  168.0 0.2 select_reduce_fusion
  168.2 86.1 %reduce-scatter.4.cloned.1.call-done = bf16[128,448]{1,0:T(8,128)(2,1)} async-done(((bf16[2048,448]{1,0:T(8,128)(2,1)}), bf16[128,448]{1,0:T(8,128)(2,1)}) %reduce-scatter.4.cloned.1.call-update) | async-done | bytes 114704
  254.2 1.0 copy.35
  255.3 0.0 copy-done.2
  255.3 0.1 multiply_reduce_fusion.1
  255.4 29.0 %psum.14 = f32[128]{0:T(128)S(1)} all-reduce(f32[128]{0:T(128)S(1)} %multiply_reduce_fusion.1), channel_id=1, replica_groups=mesh['ctx'=16,'exp'=16] {'ctx'}, use_global_device_ids=true, to_apply=%region_8.9 | all-reduce | flops 128 | bytes 1024 | tf_op jit(solution)/shard_map/psum | solution.py:92
  284.4 0.0 copy-done.4
  284.4 0.3 convolution_convert_fusion.4
  284.6 0.1 copy.30
  284.8 15.6 %all_to_all.10 = bf16[16,16,448]{2,1,0:T(8,128)(2,1)S(1)} all-to-all(bf16[16,16,448]{2,1,0:T(8,128)(2,1)S(1)} %bitcast.45), channel_id=1, replica_groups=mesh['ctx'=16,'exp'=16] {'exp'}, dimensions={0} | all-to-all | bytes 458752 | tf_op jit(solution)/shard_map/all_to_all | solution.py:112
  300.4 0.0 copy-done
  300.4 0.7 fusion.8
  301.1 2.2 fusion.9
  303.3 1.5 pad_maximum_fusion
  304.8 0.0 all-reduce.2.cloned.1.call-update
  304.9 123.2 %all-reduce.2.cloned.1.call-done = bf16[256,2,2048]{2,0,1:T(8,128)(2,1)} async-done(((bf16[256,2,2048]{2,0,1:T(8,128)(2,1)}), bf16[256,2,2048]{2,0,1:T(8,128)(2,1)}) %all-reduce.2.cloned.1.call-update) | async-done | bytes 2097168 | tf_op jit(solution)/shard_map/psum | solution.py:118
  428.1 2.2 convert_element_type.69
  430.3 0.0 copy-done.8
  430.3 0.0 copy-start.6
  430.3 0.9 fusion.40
  431.2 0.1 copy.31
  431.4 19.2 %all_to_all.11 = bf16[16,16,448]{2,1,0:T(8,128)(2,1)S(1)} all-to-all(bf16[16,16,448]{2,1,0:T(8,128)(2,1)S(1)} %bitcast.46), channel_id=1, replica_groups=mesh['ctx'=16,'exp'=16] {'exp'}, dimensions={0} | all-to-all | bytes 458752 | tf_op jit(solution)/shard_map/all_to_all | solution.py:121
  450.5 0.0 copy-done.6
  450.5 0.9 fusion.44
  (11 shorter events, 0.1 us)
Async XLA Ops:
  6.5 293.9 %copy-start = (bf16[1,448,2048]{2,1,0:T(8,128)(2,1)S(1)}, bf16[1,448,2048]{2,1,0:T(8,128)(2,1)}, u32[]{:S(2)}) copy-start(bf16[1,448,2048]{2,1,0:T(8,128)(2,1)} %param.23) | copy-start | bytes 5505028
  6.5 47.5 %all-gather.6.cloned.1.call-start = ((), (), s32[]{:S(2)}) async-start(), calls=%async_computation.4 | async-start | bytes 2506752 | tf_op jit(solution)/shard_map/all_gather | solution.py:70
  7.3 99.9 %all-gather.4.cloned.1.call-start = ((), (), s32[]{:S(2)}) async-start(), calls=%async_computation.3 | async-start | bytes 5013504 | tf_op jit(solution)/shard_map/all_gather | solution.py:67
  8.0 151.7 %all-gather.8.cloned.1.call-start = ((), (), s32[]{:S(2)}) async-start(), calls=%async_computation.5 | async-start | bytes 2228224 | tf_op jit(solution)/shard_map/all_gather | solution.py:84
  107.1 5.7 %copy-start.1 = (f32[512,2048]{1,0:T(8,128)S(1)}, f32[512,2048]{1,0:T(8,128)}, u32[]{:S(2)}) copy-start(f32[512,2048]{1,0:T(8,128)} %get-tuple-element.13) | copy-start | bytes 12582916
  112.8 2.9 slice-start
  114.2 1.5 slice-start.1
  115.7 2.5 copy-start.7
  118.2 1.7 copy-start.3
  120.9 133.3 %reduce-scatter.4.cloned.1.call-start = ((), (), s32[]{:S(2)}) async-start(), calls=%async_computation.7 | async-start | bytes 2228224
  163.8 3.9 copy-start.5
  163.8 91.5 %copy-start.2 = (bf16[128,448]{0,1:T(8,128)(2,1)S(1)}, bf16[128,448]{0,1:T(8,128)(2,1)}, u32[]{:S(2)}) copy-start(bf16[128,448]{0,1:T(8,128)(2,1)} %param.19) | copy-start | bytes 344068
  163.8 120.6 %copy-start.4 = (f32[448]{0:T(512)S(1)}, f32[448]{0:T(512)}, u32[]{:S(2)}) copy-start(f32[448]{0:T(512)} %param.20) | copy-start | bytes 5380
  167.7 260.4 %all-reduce.2.cloned.1.call-start = ((), (), s32[]{:S(2)}) async-start(), calls=%async_computation.6 | async-start | bytes 4194304 | tf_op jit(solution)/shard_map/psum | solution.py:118
  428.1 2.2 copy-start.8
  430.3 20.2 %copy-start.6 = (f32[128,1]{0,1:T(1,128)S(1)}, f32[128,1]{0,1:T(1,128)}, u32[]{:S(2)}) copy-start(f32[128,1]{0,1:T(1,128)} %param.22) | copy-start | bytes 1540
Sparse Core Ops, SparseCore 0:
  9.1 44.9 all-gather.5
  55.8 51.2 all-gather.3
  121.0 38.5 all-gather.7
  167.8 86.4 reduce-scatter.3
  305.0 123.0 all-reduce.1
where the time goes:
time: 458 us
  waiting for transfers between devices  339 us (74%)
  blocking collectives  63.8 us (14%)
  matrix products  26.9 us (6%)
  between operations  13.4 us (3%)
  local copies, waits for them, and re-layouts  7.3 us (2%)
  other arithmetic  7.17 us (2%)
    psum x1, waiting for transfers between devices, per_device(): summed = lax.psum(stacked.astype(jnp.bfloat16), 'ctx').astype(jnp.float32)  123 us
    unnamed x6, waiting for transfers between devices  87.5 us
    all_gather x1, waiting for transfers between devices, per_device(): lax.all_gather(latent_cache, 'ctx', axis=0, tiled=True)  47.3 us
    all_gather x1, waiting for transfers between devices, per_device(): piece = lax.all_gather(group_latent, 'ctx', axis=0, tiled=True)  42.6 us
    all_gather x1, waiting for transfers between devices, per_device(): gathered = lax.all_gather(per_head_output, 'ctx', axis=0, tiled=True)  38.5 us
    psum x1, blocking collectives, per_device(): square_sums = lax.psum(jnp.sum(state * state, axis=1), 'ctx')  29 us
    all_to_all x1, blocking collectives, per_device(): lax.all_to_all(expert_out.reshape(sources, slots, width), 'exp', split_ax...  19.2 us
    all_to_all x1, blocking collectives, per_device(): lax.all_to_all(outgoing, 'exp', split_axis=0, concat_axis=0, tiled=True)  15.6 us
  transfers between devices with their start and end apart: 5, of which 5 were waited for; matrix products, arithmetic and copies ran while one was open for 2% of the time, Pallas kernels for 0%

commit v1 on v0

v1 whole, which is shorter than its diff:
```python
import math

import jax
import jax.numpy as jnp
from jax import lax
from jax.experimental import pallas as pl
from jax.experimental.pallas import tpu as pltpu
from jax.sharding import PartitionSpec as P

MESH = pl.DeviceIdType.MESH
F32 = jnp.float32
BF16 = jnp.bfloat16
D = 7168
CAP = 16
HEADS = 4
TOK = 128
NOPE = 128
RANK = 512
VD = 128
WIDTH = 448
FF = 2048
HALF = FF // 2
CACHE = 256
GROUP = 128
KEYS = CACHE + GROUP
KW = RANK + 128
SCALE = 1.0 / math.sqrt(192.0) * math.log2(math.e)


def mm(a, b):
    return jnp.dot(a, b, preferred_element_type=F32)


def kernel(
    q_ref,
    cache_ref,
    group_ref,
    wk_ref,
    wv_ref,
    wo_ref,
    res_ref,
    gain_ref,
    rt_ref,
    rw_ref,
    wg_ref,
    wu_ref,
    wd_ref,
    out_ref,
    qbuf,
    kbuf,
    qabuf,
    acc,
    mbuf,
    lbuf,
    osend,
    ssend,
    orecv,
    srecv,
    agbuf,
    wbuf,
    rsend,
    rrecv,
    state,
    dsend,
    drecv,
    gubuf,
    wdbuf,
    psend,
    precv,
    hid,
    ysend,
    yrecv,
    sem_q,
    sem_k,
    sem_w,
    sem_gu,
    sem_wd,
    sem_o,
    sem_s,
    sem_ag,
    sem_f,
    sem_rs,
    sem_d,
    sem_df,
    sem_p,
    sem_h,
    sem_hf,
    sem_y,
):
    c = lax.axis_index("ctx")
    e = lax.axis_index("exp")
    x, zl, k = c // 4, (c // 2) % 2, c % 2
    y, zh = e // 4, e % 4
    z = 2 * zh + zl

    def at(x_, zl_, k_, y_, zh_):
        return (x_ * 4 + zl_ * 2 + k_, y_ * 4 + zh_)

    def at_z(z_):
        return at(x, z_ % 2, k, y, z_ // 2)

    sibling = at(x, zl, 1 - k, y, zh)
    z_up = at_z((z + 1) % 8)
    z_down = at_z((z + 7) % 8)
    diagonal = x == y

    def remote(src, dst, sems, i, device):
        return pltpu.make_async_remote_copy(
            src_ref=src,
            dst_ref=dst,
            send_sem=sems.at[0, i],
            recv_sem=sems.at[1, i],
            device_id=device,
            device_id_type=MESH,
        )

    barrier = pltpu.get_barrier_semaphore()

    def hello(device):
        pl.semaphore_signal(barrier, inc=1, device_id=device, device_id_type=MESH)

    for d in (1, 3, 2):
        hello(at((x + d) % 4, zl, k, y, zh))
        hello(at(x, zl, k, (y + d) % 4, zh))
    hello(sibling)
    hello(z_up)
    hello(z_down)
    hello(at(x, zl, k, y, (zh + 2) % 4))
    for j in range(4):

        @pl.when(jnp.logical_not(jnp.logical_and(diagonal, x == j)))
        def _():
            hello(at(j, zl, k, x, zh))

    for rows, ref in ((0, cache_ref), (CACHE, group_ref)):
        count = ref.shape[0]
        kbuf[0, rows : rows + count, 0:RANK] = ref[:, 0:RANK]
        rope = ref[:, RANK:]
        kbuf[0, rows : rows + count, RANK:KW] = jnp.concatenate([rope, rope], axis=1)
    qbuf[0] = q_ref[...]

    pl.semaphore_wait(barrier, jnp.where(diagonal, 13, 14))

    q_copies = {}
    for d in (1, 3, 2):
        q_copies[d] = remote(
            q_ref, qbuf.at[d], sem_q, d, at((x + 4 - d) % 4, zl, k, y, zh)
        )
    half = KEYS // 2
    k_up = remote(
        kbuf.at[0, 0:half], kbuf.at[1, 0:half], sem_k, 0, z_up
    )
    k_down = remote(
        kbuf.at[0, half:KEYS], kbuf.at[1, half:KEYS], sem_k, 1, z_down
    )
    k_sib = remote(
        kbuf.at[0, 0:KEYS], kbuf.at[0, KEYS : 2 * KEYS], sem_k, 2, sibling
    )
    f_up = remote(
        kbuf.at[1, 0:half], kbuf.at[1, KEYS : KEYS + half], sem_k, 3, sibling
    )
    f_down = remote(
        kbuf.at[1, half:KEYS], kbuf.at[1, KEYS + half : 2 * KEYS], sem_k, 4, sibling
    )
    k_sib.start()
    q_copies[1].start()
    q_copies[3].start()
    k_up.start()
    k_down.start()
    q_copies[2].start()

    w_copies = [
        remote(wo_ref, wbuf.at[d], sem_w, d, at(x, zl, k, (y + 4 - d) % 4, zh))
        for d in (1, 3, 2)
    ]
    w_own = pltpu.make_async_copy(wo_ref, wbuf.at[0], sem_w.at[0, 0])
    for copy in w_copies:
        copy.start()
    w_own.start()
    mine = pl.ds(pl.multiple_of(k * HALF, 128), HALF)
    other = pl.ds(pl.multiple_of((1 - k) * HALF, 128), HALF)
    gu_remote = []
    gu_local = []
    for i, ref in enumerate((wg_ref, wu_ref)):
        lanes = pl.ds(i * HALF, HALF)
        gu_remote.append(
            remote(ref.at[0, :, other], gubuf.at[1, :, lanes], sem_gu, i, sibling)
        )
        gu_local.append(
            pltpu.make_async_copy(
                ref.at[0, :, mine], gubuf.at[0, :, lanes], sem_gu.at[0, 2 + i]
            )
        )
    wd_copy = pltpu.make_async_copy(wd_ref.at[0], wdbuf, sem_wd)
    for copy in gu_local + gu_remote + [wd_copy]:
        copy.start()

    lane = lax.broadcasted_iota(jnp.int32, (TOK, 128), 1)
    row = lax.broadcasted_iota(jnp.int32, (TOK, 128), 0)
    ahead = lane - row
    ahead2 = jnp.concatenate([ahead, ahead], axis=0)

    def scores(d, pair, side):
        queries = qabuf[d, pair * 256 : pair * 256 + 256, :]
        s = (
            lax.dot_general(
                queries,
                kbuf[side],
                (((1,), (1,)), ((), ())),
                preferred_element_type=F32,
            )
            * SCALE
        )
        token_block = 4 * ((x + d) % 4) + 2 * zl + k
        zl_key = zl if side == 0 else 1 - zl
        parts = []
        for slot in range(2):
            k_key = k if slot == 0 else 1 - k
            key_block = 4 * x + 2 * zl_key + k_key
            base = slot * KEYS
            parts.append(s[:, base : base + CACHE])
            parts.append(
                jnp.where(
                    ahead2 <= (token_block - key_block) * TOK,
                    s[:, base + CACHE : base + KEYS],
                    -1e30,
                )
            )
        return jnp.concatenate(parts, axis=1)

    def first_half(i, carry):
        d = i ^ (i // 2)

        @pl.when(i > 0)
        def _():
            remote(q_ref, qbuf.at[d], sem_q, d, sibling).wait_recv()

        for h in range(HEADS):
            lowered = mm(qbuf[d, h], wk_ref[h]).astype(BF16)
            tile = qbuf[d, HEADS + h // 2]
            keep = lane < 64 if h % 2 == 0 else lane >= 64
            qabuf[d, h * TOK : (h + 1) * TOK, 0:RANK] = lowered
            qabuf[d, h * TOK : (h + 1) * TOK, RANK:KW] = jnp.where(
                keep, tile, jnp.zeros_like(tile)
            )

        @pl.when(i == 0)
        def _():
            k_sib.wait_recv()

        for pair in range(2):
            rows = slice(pair * 256, pair * 256 + 256)
            s = scores(d, pair, 0)
            m = jnp.max(s, axis=1, keepdims=True)
            p = jnp.exp2(s - m)
            mbuf[d, rows, :] = m
            lbuf[d, rows, :] = jnp.sum(p, axis=1, keepdims=True)
            acc[d, rows, :] = mm(p.astype(BF16), kbuf[0, :, 0:RANK])

        @pl.when(i == 1)
        def _():
            k_up.wait_recv()
            f_up.start()
            k_down.wait_recv()
            f_down.start()

        return carry

    lax.fori_loop(0, 4, first_half, 0)
    f_up.wait_recv()
    f_down.wait_recv()

    def o_copies(d):
        token_x = (x + d) % 4
        device = at(y, zl, k, token_x, zh)
        return (
            remote(osend.at[d], orecv.at[x], sem_o, x, device),
            remote(ssend.at[d], srecv.at[x], sem_s, x, device),
        )

    def o_local(d):
        return (
            pltpu.make_async_copy(osend.at[d], orecv.at[x], sem_o.at[1, x]),
            pltpu.make_async_copy(ssend.at[d], srecv.at[x], sem_s.at[1, x]),
        )

    def second_half(i, carry):
        d = i ^ (i // 2)
        stats = jnp.zeros((TOK, 128), F32)
        for pair in range(2):
            rows = slice(pair * 256, pair * 256 + 256)
            s = scores(d, pair, 1)
            m_old = mbuf[d, rows, :]
            m = jnp.maximum(m_old, jnp.max(s, axis=1, keepdims=True))
            p = jnp.exp2(s - m)
            decay = jnp.exp2(m_old - m)
            total = lbuf[d, rows, :] * decay + jnp.sum(p, axis=1, keepdims=True)
            numerator = acc[d, rows, :] * decay + mm(
                p.astype(BF16), kbuf[1, :, 0:RANK]
            )
            context = (numerator / total).astype(BF16)
            lse = m + jnp.log2(total)
            for j in range(2):
                h = pair * 2 + j
                part = slice(j * TOK, (j + 1) * TOK)
                osend[d, :, h * VD : (h + 1) * VD] = mm(
                    context[part], wv_ref[h]
                ).astype(BF16)
                stats = jnp.where(lane == h, lse[part], stats)
        ssend[d] = stats.T[0:8]
        on_self = jnp.logical_and(diagonal, i == 0)

        @pl.when(on_self)
        def _():
            for copy in o_local(d):
                copy.start()

        @pl.when(jnp.logical_not(on_self))
        def _():
            for copy in o_copies(d):
                copy.start()

        return carry

    lax.fori_loop(0, 4, second_half, 0)

    for j in range(4):
        pltpu.make_async_copy(osend.at[0], orecv.at[j], sem_o.at[1, j]).wait()
        pltpu.make_async_copy(ssend.at[0], srecv.at[j], sem_s.at[1, j]).wait()
    lses = [srecv[j] for j in range(4)]
    top = jnp.maximum(jnp.maximum(lses[0], lses[1]), jnp.maximum(lses[2], lses[3]))
    shares = [jnp.exp2(lse - top) for lse in lses]
    whole = shares[0] + shares[1] + shares[2] + shares[3]
    shares = [share / whole for share in shares]
    weights = jnp.concatenate(shares + [jnp.zeros((96, 128), F32)], axis=0).T
    for h in range(HEADS):
        lanes = slice(h * VD, (h + 1) * VD)
        merged = jnp.zeros((TOK, VD), F32)
        for j in range(4):
            merged += weights[:, 8 * j + h : 8 * j + h + 1] * orecv[
                j, :, lanes
            ].astype(F32)
        agbuf[c, :, lanes] = merged.astype(BF16)

    chips = [(0, 1), (1, 0), (3, 0), (1, 1), (3, 1), (2, 0), (2, 1)]

    def ag_source(dx, dz):
        return ((x + 4 - dx) % 4) * 4 + ((zl + dz) % 2) * 2 + k

    ag_copies = []
    for i, (dx, dz) in enumerate(chips):
        copy = remote(
            agbuf.at[c],
            agbuf.at[c],
            sem_ag,
            i,
            at((x + dx) % 4, (zl + dz) % 2, k, y, zh),
        )
        copy.start()
        ag_copies.append(copy)
    forwards = [remote(agbuf.at[c], agbuf.at[c], sem_f, 7, sibling)]
    forwards[0].start()
    for i, (dx, dz) in enumerate(chips):
        source = ag_source(dx, dz)
        remote(agbuf.at[source], agbuf.at[source], sem_ag, i, sibling).wait_recv()
        copy = remote(agbuf.at[source], agbuf.at[source], sem_f, i, sibling)
        copy.start()
        forwards.append(copy)
    for i, (dx, dz) in enumerate(chips):
        source = ag_source(dx, dz) + 1 - 2 * k
        remote(agbuf.at[source], agbuf.at[source], sem_f, i, sibling).wait_recv()
    source = c + 1 - 2 * k
    remote(agbuf.at[source], agbuf.at[source], sem_f, 7, sibling).wait_recv()

    for copy in w_copies:
        copy.wait_recv()
    w_own.wait()

    def project(j):
        total = jnp.zeros((TOK, WIDTH), F32)
        for dy in range(4):
            total += mm(agbuf[4 * ((y + dy) % 4) + j], wbuf[dy])
        return total

    rs_copies = []
    for i, d in enumerate((2, 1, 3)):
        j = (zh + d) % 4
        rsend[i] = project(j).astype(BF16)
        copy = remote(rsend.at[i], rrecv.at[i], sem_rs, i, at(x, zl, k, y, j))
        copy.start()
        rs_copies.append(copy)
    total = project(zh) + res_ref[...].astype(F32)

    expert = jnp.broadcast_to(rt_ref[...], (TOK, TOK))
    expert_row = jnp.sum(
        jnp.where(lane == row, expert, 0), axis=0, keepdims=True
    )
    earlier = jnp.sum(
        jnp.where(jnp.logical_and(expert == expert_row, row < lane), 1, 0),
        axis=0,
        keepdims=True,
    )
    target = expert_row * CAP + earlier
    slots = lax.broadcasted_iota(jnp.int32, (2 * TOK, TOK), 0)
    select = jnp.where(slots == target, 1.0, 0.0).astype(BF16)

    for copy in rs_copies:
        copy.wait_recv()
    for i in range(3):
        total += rrecv[i].astype(F32)
    state[...] = total

    squares = jnp.sum(total * total, axis=1, keepdims=True)
    high = squares.astype(BF16)
    rest = squares - high.astype(F32)
    middle = rest.astype(BF16)
    low = (rest - middle.astype(F32)).astype(BF16)
    pairs = (total * gain_ref[...]).astype(BF16)
    terms = jnp.where(
        lane == 0,
        high.astype(F32),
        jnp.where(
            lane == 1, middle.astype(F32), jnp.where(lane == 2, low.astype(F32), 0.0)
        ),
    ).astype(BF16)
    dsend[:, 0:WIDTH] = mm(select, pairs).astype(BF16)
    dsend[:, 512:640] = mm(select, terms).astype(BF16)
    experts = [(dy, dz) for dy in range(4) for dz in range(4)][1:]
    d_copies = []
    for i, (dy, dz) in enumerate(experts):
        peer = 4 * ((y + dy) % 4) + (zh + dz) % 4
        copy = remote(
            dsend.at[pl.ds(peer * CAP, CAP)],
            drecv.at[0, pl.ds(e * CAP, CAP)],
            sem_d,
            i,
            (c, peer),
        )
        copy.start()
        d_copies.append(copy)
    own_rows = pl.ds(pl.multiple_of(e * CAP, CAP), CAP)
    drecv[0, own_rows, :] = dsend[own_rows, :]
    for copy in d_copies:
        copy.wait_recv()
    d_forward = remote(drecv.at[0], drecv.at[1], sem_df, 0, sibling)
    d_forward.start()

    for copy in gu_local:
        copy.wait()
    for copy in gu_remote:
        copy.wait_recv()
    d_forward.wait_recv()
    rows0 = drecv[0, :, 0:WIDTH]
    rows1 = drecv[1, :, 0:WIDTH]
    for col in range(4):
        lanes = slice(col * 512, (col + 1) * 512)
        psend[:, lanes] = (
            mm(rows0, gubuf[0, :, lanes]) + mm(rows1, gubuf[1, :, lanes])
        ).astype(BF16)
    tail = drecv[0, :, 512:640].astype(F32) + drecv[1, :, 512:640].astype(F32)
    row_squares = jnp.sum(tail, axis=1, keepdims=True)
    high = row_squares.astype(BF16)
    rest = row_squares - high.astype(F32)
    middle = rest.astype(BF16)
    low = (rest - middle.astype(F32)).astype(BF16)
    lane2 = lax.broadcasted_iota(jnp.int32, (256, 128), 1)
    psend[:, FF : FF + 128] = jnp.where(
        lane2 == 0,
        high.astype(F32),
        jnp.where(
            lane2 == 1,
            middle.astype(F32),
            jnp.where(lane2 == 2, low.astype(F32), 0.0),
        ),
    ).astype(BF16)

    chip = 2 * x + zl
    order = [(2, 1), (2, 0), (1, 1), (3, 1), (1, 0), (3, 0), (0, 1)]
    p_copies = []
    for i, (dx, dz) in enumerate(order):
        px, pz = (x + dx) % 4, (zl + dz) % 2
        copy = remote(
            psend.at[pl.ds((2 * px + pz) * 32, 32)],
            precv.at[i],
            sem_p,
            i,
            at(px, pz, k, y, zh),
        )
        copy.start()
        p_copies.append(copy)
    own32 = pl.ds(pl.multiple_of(chip * 32, 32), 32)
    summed = psend[own32, :].astype(F32)
    for i in (6, 4, 5, 2, 3, 1, 0):
        p_copies[i].wait_recv()
        summed += precv[i].astype(F32)
    mean = jnp.sum(summed[:, FF : FF + 128], axis=1, keepdims=True) / D
    factor = lax.rsqrt(mean + 1e-6)
    gate = summed[:, 0:HALF] * factor
    up = summed[:, HALF:FF] * factor
    hid[0, own32, :] = (gate / (1.0 + jnp.exp(-gate)) * up).astype(BF16)

    h_copies = []
    for i, (dx, dz) in enumerate(chips):
        copy = remote(
            hid.at[0, pl.ds(chip * 32, 32)],
            hid.at[0, pl.ds(chip * 32, 32)],
            sem_h,
            i,
            at((x + dx) % 4, (zl + dz) % 2, k, y, zh),
        )
        copy.start()
        h_copies.append(copy)

    def hid_rows(index, dx, dz):
        source = 2 * ((x + 4 - dx) % 4) + (zl + dz) % 2
        return hid.at[index, pl.ds(source * 32, 32)]

    hf_copies = [remote(hid_rows(0, 0, 0), hid_rows(1, 0, 0), sem_hf, 7, sibling)]
    hf_copies[0].start()
    for i, (dx, dz) in enumerate(chips):
        remote(hid_rows(0, dx, dz), hid_rows(0, dx, dz), sem_h, i, sibling).wait_recv()
        copy = remote(hid_rows(0, dx, dz), hid_rows(1, dx, dz), sem_hf, i, sibling)
        copy.start()
        hf_copies.append(copy)
    wd_copy.wait()
    down = mm(hid[0], wdbuf[pl.ds(pl.multiple_of(k * HALF, HALF), HALF), :])
    for copy in hf_copies:
        copy.wait_recv()
    down += mm(hid[1], wdbuf[pl.ds(pl.multiple_of((1 - k) * HALF, HALF), HALF), :])
    ysend[...] = down.astype(BF16)

    y_copies = []
    for i, (dy, dz) in enumerate(experts):
        peer = 4 * ((y + dy) % 4) + (zh + dz) % 4
        copy = remote(
            ysend.at[pl.ds(peer * CAP, CAP)],
            yrecv.at[pl.ds(e * CAP, CAP)],
            sem_y,
            i,
            (c, peer),
        )
        copy.start()
        y_copies.append(copy)
    yrecv[own_rows, :] = ysend[own_rows, :]
    for copy in y_copies:
        copy.wait_recv()
    routed = lax.dot_general(
        select, yrecv[...], (((0,), (0,)), ((), ())), preferred_element_type=F32
    )
    out_ref[...] = (state[...] + routed * rw_ref[...]).astype(BF16)

    for d in (1, 2, 3):
        q_copies[d].wait_send()
    for copy in (k_up, k_down, k_sib, f_up, f_down):
        copy.wait_send()
    for copy in w_copies + gu_remote:
        copy.wait_send()
    for d in range(4):
        if d == 0:

            @pl.when(jnp.logical_not(diagonal))
            def _():
                for copy in o_copies(0):
                    copy.wait_send()

        else:
            for copy in o_copies(d):
                copy.wait_send()
    for copy in (
        ag_copies
        + forwards
        + rs_copies
        + d_copies
        + [d_forward]
        + p_copies
        + h_copies
        + hf_copies
        + y_copies
    ):
        copy.wait_send()


def per_device(
    queries,
    latent_cache,
    group_latent,
    w_absorb_k,
    value_absorb_weight,
    w_out,
    residual,
    norm_gain,
    routes,
    route_weight,
    w_gate,
    w_up,
    w_down,
):
    rope = queries[:, :, NOPE:].reshape(TOK, 2, 128)
    packed = jnp.concatenate([queries[:, :, :NOPE], rope], axis=1).transpose(1, 0, 2)
    vmem = pl.BlockSpec(memory_space=pltpu.VMEM)
    hbm = pl.BlockSpec(memory_space=pl.ANY)
    dma = pltpu.SemaphoreType.DMA
    return pl.pallas_call(
        kernel,
        out_shape=jax.ShapeDtypeStruct((TOK, WIDTH), BF16),
        in_specs=[vmem] * 5 + [hbm] + [vmem] * 4 + [hbm] * 3,
        out_specs=vmem,
        scratch_shapes=[
            pltpu.VMEM((4, 6, TOK, 128), BF16),
            pltpu.VMEM((2, 2 * KEYS, KW), BF16),
            pltpu.VMEM((4, HEADS * TOK, KW), BF16),
            pltpu.VMEM((4, HEADS * TOK, RANK), F32),
            pltpu.VMEM((4, HEADS * TOK, 1), F32),
            pltpu.VMEM((4, HEADS * TOK, 1), F32),
            pltpu.VMEM((4, TOK, HEADS * VD), BF16),
            pltpu.VMEM((4, 8, 128), F32),
            pltpu.VMEM((4, TOK, HEADS * VD), BF16),
            pltpu.VMEM((4, 8, 128), F32),
            pltpu.VMEM((16, TOK, HEADS * VD), BF16),
            pltpu.VMEM((4, HEADS * VD, WIDTH), BF16),
            pltpu.VMEM((3, TOK, WIDTH), BF16),
            pltpu.VMEM((3, TOK, WIDTH), BF16),
            pltpu.VMEM((TOK, WIDTH), F32),
            pltpu.VMEM((2 * TOK, 640), BF16),
            pltpu.VMEM((2, 2 * TOK, 640), BF16),
            pltpu.VMEM((2, WIDTH, FF), BF16),
            pltpu.VMEM((FF, WIDTH), BF16),
            pltpu.VMEM((2 * TOK, FF + 128), BF16),
            pltpu.VMEM((7, 32, FF + 128), BF16),
            pltpu.VMEM((2, 2 * TOK, HALF), BF16),
            pltpu.VMEM((2 * TOK, WIDTH), BF16),
            pltpu.VMEM((2 * TOK, WIDTH), BF16),
            dma((2, 4)),
            dma((2, 5)),
            dma((2, 4)),
            dma((2, 4)),
            dma,
            dma((2, 4)),
            dma((2, 4)),
            dma((2, 7)),
            dma((2, 8)),
            dma((2, 3)),
            dma((2, 15)),
            dma((2, 1)),
            dma((2, 7)),
            dma((2, 7)),
            dma((2, 8)),
            dma((2, 15)),
        ],
        compiler_params=pltpu.CompilerParams(
            collective_id=0, has_side_effects=True, vmem_limit_bytes=56 * 2**20
        ),
        name="layer",
    )(
        packed,
        latent_cache,
        group_latent,
        w_absorb_k,
        value_absorb_weight,
        w_out,
        residual,
        norm_gain.reshape(1, WIDTH),
        routes,
        route_weight,
        w_gate,
        w_up,
        w_down,
    )


def solution(mesh):
    in_specs = (
        P("ctx", "exp", None),
        P("ctx", None),
        P("ctx", None),
        P("exp", None, None),
        P("exp", None, None),
        P("exp", "ctx"),
        P("exp", "ctx"),
        P("ctx"),
        P("exp", None),
        P("exp", None),
        P("exp", "ctx", None),
        P("exp", "ctx", None),
        P("exp", None, "ctx"),
    )
    out_specs = P("exp", "ctx")
    return jax.shard_map(
        per_device, mesh=mesh, in_specs=in_specs, out_specs=out_specs, check_vma=False
    )
```

time: 458 us -> 161 us (0.35)
  waiting for transfers between devices: 339 us -> 0 us
  Pallas kernels: 0 us -> 143 us
  blocking collectives: 63.8 us -> 0 us
  matrix products: 26.9 us -> 0 us
  between operations: 13.4 us -> 0.03 us
  local copies, waits for them, and re-layouts: 7.3 us -> 15.2 us
  other arithmetic: 7.17 us -> 0.71 us
    pallas_call x0 -> x1, Pallas kernels: none -> 143 us  [per_device(): pl.pallas_call(kernel, out_shape=jax.ShapeDtypeStruct((TOK, WIDTH), BF16)...]
    all_gather x3 -> x0, waiting for transfers between devices: 128 us -> none  [the longest x1 47.3 us: per_device(): lax.all_gather(latent_cache, 'ctx', axis=0, tiled=True)]
    psum x1 -> x0, waiting for transfers between devices: 123 us -> none  [per_device(): summed = lax.psum(stacked.astype(jnp.bfloat16), 'ctx').astype(jnp.float32)]
    unnamed x6 -> x0, waiting for transfers between devices: 87.5 us -> none
    all_to_all x2 -> x0, blocking collectives: 34.8 us -> none  [the longest x1 19.2 us: per_device(): lax.all_to_all(expert_out.reshape(sources, slots, width), 'exp', split_ax...]
    psum x1 -> x0, blocking collectives: 29 us -> none  [per_device(): square_sums = lax.psum(jnp.sum(state * state, axis=1), 'ctx')]
    dot_general x12 -> x0, matrix products: 26.9 us -> none  [the longest x2 11.4 us: fold_keys(): lax.dot_general(absorbed_query, piece, (((1,), (1,)), ((), ())), preferre...]
    unnamed x24 -> x12, local copies, waits for them, and re-layouts: 4.94 us -> 11.7 us
  transfers between devices with their start and end apart: 5 -> 0, of which waited for: 5 -> 0; matrix products, arithmetic and copies ran while one was open for 2% -> 0% of each run, Pallas kernels for 0% -> 0%
where the time goes in v1:
time: 161 us; the launch traced here: 159 us
  Pallas kernels  143 us (89%)
  local copies, waits for them, and re-layouts  15.2 us (9%)
    pallas_call x1, Pallas kernels, per_device(): pl.pallas_call(kernel, out_shape=jax.ShapeDtypeStruct((TOK, WIDTH), BF16)...  143 us
    unnamed x12, local copies, waits for them, and re-layouts  11.7 us

profile of v1, /device:TPU:1, one launch (start us, length us, event | category | flops | bytes accessed | tf_op | source)
XLA Modules:
  0.0 159.0 jit_solution(16970640116100793057)
XLA Ops:
  0.0 0.0 copy-start
  0.0 0.0 copy-start.1
  0.0 1.5 copy.29.rt_ref
  1.5 1.4 copy.30.rw_ref
  2.9 0.8 slice.7
  3.8 0.1 copy.24
  3.9 1.6 %copy.28.res_ref = bf16[128,448]{1,0:T(8,128)(2,1)} copy(bf16[128,448]{0,1:T(8,128)(2,1)} %param.19) | data formatting | bytes 229376 | tf_op args[6]
  5.5 0.9 slice.6
  6.5 0.1 copy.33
  6.6 0.7 maximum_bitcast_fusion.q_ref
  7.3 1.7 %copy.26.group_ref = bf16[128,576]{1,0:T(8,128)(2,1)} copy(bf16[128,576]{0,1:T(8,128)(2,1)} %param.15) | data formatting | bytes 294912 | tf_op args[2]
  9.0 1.9 %copy.25.cache_ref = bf16[256,576]{1,0:T(8,128)(2,1)} copy(bf16[256,576]{0,1:T(8,128)(2,1)} %param.14) | data formatting | bytes 589824 | tf_op args[1]
  10.9 0.0 copy-done.1
  10.9 1.0 copy.27.wo_ref
  11.9 0.0 copy-done
  11.9 2.4 %copy.31.wd_ref = bf16[1,2048,448]{2,1,0:T(8,128)(2,1)} copy(bf16[1,2048,448]{1,2,0:T(8,128)(2,1)S(1)} %copy-done) | data formatting | bytes 3670016 | tf_op args[12]
  14.3 143.1 %layer.1 = bf16[128,448]{1,0:T(8,128)(2,1)} custom-call(bf16[6,128,128]{2,1,0:T(8,128)(2,1)} %maximum_bitcast_fusion.q_ref, bf16[256,576]{1,0:T(8,128)(2,1)} %copy.25.cache_ref, bf16[128,576]{1,0:T(8,128)(2,1)} %copy.26.group_ref, bf16[4,128,512]{2,1,0:T(8,128)(2,1)} %wk_ref.1, bf16[4,512,128]{2,1,0:T(8,128)(2,1)} %wv_ref.1, bf16[512,448]{1,0:T(8,128)(2,1)} %copy.27.wo_ref, ...), custom_call_target="tpu_custom_call" | custom-call | tf_op jit(solution)/shard_map/layer/pallas_call | solution.py:603
  157.4 1.7 %copy.32 = bf16[128,448]{0,1:T(8,128)(2,1)} copy(bf16[128,448]{1,0:T(8,128)(2,1)} %layer.1) | data formatting | bytes 229376 | tf_op jit(solution)/shard_map/layer/pallas_call | solution.py:603
Async XLA Ops:
  0.0 11.9 %copy-start = (bf16[1,2048,448]{1,2,0:T(8,128)(2,1)S(1)}, bf16[1,2048,448]{1,2,0:T(8,128)(2,1)}, u32[]{:S(2)}) copy-start(bf16[1,2048,448]{1,2,0:T(8,128)(2,1)} %param.25) | copy-start | bytes 5505028
  0.0 10.9 %copy-start.1 = (bf16[512,448]{0,1:T(8,128)(2,1)S(1)}, bf16[512,448]{0,1:T(8,128)(2,1)}, u32[]{:S(2)}) copy-start(bf16[512,448]{0,1:T(8,128)(2,1)} %param.18) | copy-start | bytes 1376260

commit v2 on v0

v2 whole, which is shorter than its diff:
```python
import math

import jax
import jax.numpy as jnp
from jax import lax
from jax.experimental import pallas as pl
from jax.experimental.pallas import tpu as pltpu
from jax.sharding import PartitionSpec as P

MESH = pl.DeviceIdType.MESH
F32 = jnp.float32
BF16 = jnp.bfloat16
D = 7168
CAP = 16
HEADS = 4
TOK = 128
NOPE = 128
RANK = 512
VD = 128
WIDTH = 448
FF = 2048
HALF = FF // 2
CACHE = 256
GROUP = 128
KEYS = CACHE + GROUP
KW = RANK + 128
SCALE = 1.0 / math.sqrt(192.0) * math.log2(math.e)


def mm(a, b):
    return jnp.dot(a, b, preferred_element_type=F32)


def mm_t(a, b):
    return lax.dot_general(a, b, (((1,), (1,)), ((), ())), preferred_element_type=F32)


def kernel(
    q_ref,
    cache_ref,
    group_ref,
    wk_ref,
    wv_ref,
    wo_ref,
    res_ref,
    gain_ref,
    rt_ref,
    rw_ref,
    wg_ref,
    wu_ref,
    wd_ref,
    out_ref,
    qbuf,
    kbuf,
    qabuf,
    acc,
    mbuf,
    lbuf,
    osend,
    ssend,
    orecv,
    srecv,
    agbuf,
    wbuf,
    product,
    rsend,
    rrecv,
    state,
    pairs,
    dsend,
    drecv,
    gubuf,
    wdbuf,
    psend,
    precv,
    hid,
    ysend,
    yrecv,
    sem_q,
    sem_k,
    sem_w,
    sem_gu,
    sem_wd,
    sem_o,
    sem_s,
    sem_ag,
    sem_f,
    sem_rs,
    sem_d,
    sem_df,
    sem_p,
    sem_h,
    sem_hf,
    sem_y,
):
    c = lax.axis_index("ctx")
    e = lax.axis_index("exp")
    x, zl, k = c // 4, (c // 2) % 2, c % 2
    y, zh = e // 4, e % 4
    z = 2 * zh + zl

    def at(x_, zl_, k_, y_, zh_):
        return (x_ * 4 + zl_ * 2 + k_, y_ * 4 + zh_)

    def at_z(z_):
        return at(x, z_ % 2, k, y, z_ // 2)

    def aligned(start, size):
        return pl.ds(pl.multiple_of(start, size), size)

    sibling = at(x, zl, 1 - k, y, zh)
    z_up = at_z((z + 1) % 8)
    z_down = at_z((z + 7) % 8)
    fixed = x == (2 * y) % 4

    def remote(src, dst, sems, i, device, j=None):
        return pltpu.make_async_remote_copy(
            src_ref=src,
            dst_ref=dst,
            send_sem=sems.at[0, i],
            recv_sem=sems.at[1, i if j is None else j],
            device_id=device,
            device_id_type=MESH,
        )

    barrier = pltpu.get_barrier_semaphore()

    def hello(device):
        pl.semaphore_signal(barrier, inc=1, device_id=device, device_id_type=MESH)

    hello(at(x, zl, k, y, (zh + 2) % 4))
    for d in (2, 1, 3):
        hello(at((x + d) % 4, zl, k, y, zh))
        hello(at(x, zl, k, (y + d) % 4, zh))
    for j in range(4):

        @pl.when(jnp.logical_not(jnp.logical_and(fixed, x == j)))
        def _():
            hello(at(j, zl, k, (x + 4 - y) % 4, zh))

    hello(z_up)
    hello(z_down)
    hello(sibling)

    kbuf[0, 0 : RANK + 64, 0:CACHE] = cache_ref[...]
    kbuf[0, RANK + 64 : KW, 0:CACHE] = cache_ref[RANK:, :]
    kbuf[0, 0 : RANK + 64, CACHE:KEYS] = group_ref[...]
    kbuf[0, RANK + 64 : KW, CACHE:KEYS] = group_ref[RANK:, :]
    for h in range(HEADS):
        qbuf[0, h] = q_ref[h, 0:NOPE, :].T
    for h in range(0, HEADS, 2):
        qbuf[0, HEADS + h // 2] = jnp.concatenate(
            [q_ref[h, NOPE:, :], q_ref[h + 1, NOPE:, :]], axis=0
        ).T

    pl.semaphore_wait(barrier, jnp.where(fixed, 13, 14))

    q_copies = {}
    for d in (1, 3, 2):
        q_copies[d] = remote(
            qbuf.at[0], qbuf.at[d], sem_q, d, at((x + 4 - d) % 4, zl, k, y, zh)
        )
    first, second = slice(0, KW // 2), slice(KW // 2, KW)
    own, others = slice(0, KEYS), slice(KEYS, 2 * KEYS)
    k_up = remote(kbuf.at[0, first, own], kbuf.at[1, first, own], sem_k, 0, z_up)
    k_down = remote(kbuf.at[0, second, own], kbuf.at[1, second, own], sem_k, 1, z_down)
    k_sib = remote(kbuf.at[0, :, own], kbuf.at[0, :, others], sem_k, 2, sibling)
    f_up = remote(kbuf.at[1, first, own], kbuf.at[1, first, others], sem_k, 3, sibling)
    f_down = remote(
        kbuf.at[1, second, own], kbuf.at[1, second, others], sem_k, 4, sibling
    )
    k_sib.start()
    q_copies[1].start()
    q_copies[3].start()
    k_up.start()
    k_down.start()
    q_copies[2].start()

    w_copies = [
        remote(wo_ref, wbuf.at[d], sem_w, d, at(x, zl, k, (y + 4 - d) % 4, zh))
        for d in (1, 3, 2)
    ]
    w_own = pltpu.make_async_copy(wo_ref, wbuf.at[0], sem_w.at[0, 0])
    w_copies[0].start()
    w_copies[1].start()
    w_own.start()
    mine, other = aligned(k * HALF, HALF), aligned((1 - k) * HALF, HALF)
    gu_remote = []
    gu_local = []
    for i, ref in enumerate((wg_ref, wu_ref)):
        lanes = pl.ds(i * HALF, HALF)
        gu_remote.append(
            remote(ref.at[0, :, other], gubuf.at[1, :, lanes], sem_gu, i, sibling)
        )
        gu_local.append(
            pltpu.make_async_copy(
                ref.at[0, :, mine], gubuf.at[0, :, lanes], sem_gu.at[0, 2 + i]
            )
        )
    wd_copy = pltpu.make_async_copy(wd_ref.at[0], wdbuf, sem_wd)
    for copy in gu_local + gu_remote + [wd_copy]:
        copy.start()

    def w_ready():
        for copy in w_copies:
            copy.wait_recv()
        w_own.wait()

    def gu_ready():
        for copy in gu_local:
            copy.wait()
        for copy in gu_remote:
            copy.wait_recv()

    background = {"w": w_ready, "gu": gu_ready, "wd": wd_copy.wait}
    sent = [q_copies[1], q_copies[2], q_copies[3], k_up, k_down, k_sib]
    sent += w_copies + gu_remote
    state[...] = res_ref[...].astype(F32).T

    lane = lax.broadcasted_iota(jnp.int32, (TOK, 128), 1)
    row = lax.broadcasted_iota(jnp.int32, (TOK, 128), 0)
    lane2 = lax.broadcasted_iota(jnp.int32, (2 * TOK, 128), 1)
    ahead = lane2 - lax.broadcasted_iota(jnp.int32, (2 * TOK, 128), 0) % 64

    def scores(d, part, side):
        s = mm(qabuf[d, part], kbuf[side])
        token_block = 4 * ((x + d) % 4) + 2 * zl + k
        zl_key = zl if side == 0 else 1 - zl
        parts = []
        for slot in range(2):
            k_key = k if slot == 0 else 1 - k
            key_block = 4 * x + 2 * zl_key + k_key
            base = slot * KEYS
            parts.append(s[:, base : base + CACHE])
            parts.append(
                jnp.where(
                    ahead <= (token_block - key_block) * TOK + 64 * part,
                    s[:, base + CACHE : base + KEYS],
                    -1e30,
                )
            )
        return jnp.concatenate(parts, axis=1)

    def values(p, side):
        return mm_t(p.astype(BF16), kbuf[side, 0:RANK, :])

    def o_copies(d, part):
        token_x = (x + d) % 4
        device = at((token_x + y) % 4, zl, k, token_x, zh)
        i, j = part * 4 + d, part * 4 + x
        return (
            remote(osend.at[part, d], orecv.at[part, x], sem_o, i, device, j),
            remote(ssend.at[part, d], srecv.at[part, x], sem_s, i, device, j),
        )

    def on_self(d):
        return jnp.logical_and(fixed, (x + d) % 4 == y)

    def finish(d, part, numerator, total, m):
        context = (numerator / total).astype(BF16)
        lse = m + jnp.log2(total)
        stats = jnp.zeros((64, 128), F32)
        for h in range(HEADS):
            rows = slice(h * 64, (h + 1) * 64)
            osend[part, d, :, h * VD : (h + 1) * VD] = mm(
                context[rows], wv_ref[h]
            ).astype(BF16)
            stats = jnp.where(lane[0:64] == h, lse[rows], stats)
        ssend[part, d] = jnp.concatenate([stats, stats], axis=0).T[0:8]

        @pl.when(on_self(d))
        def _():
            j = part * 4 + x
            pltpu.make_async_copy(
                osend.at[part, d], orecv.at[part, x], sem_o.at[1, j]
            ).start()
            pltpu.make_async_copy(
                ssend.at[part, d], srecv.at[part, x], sem_s.at[1, j]
            ).start()

        @pl.when(jnp.logical_not(on_self(d)))
        def _():
            for copy in o_copies(d, part):
                copy.start()

    def near_keys(i, carry):
        d = i ^ (i // 2)

        @pl.when(i > 0)
        def _():
            remote(qbuf.at[0], qbuf.at[d], sem_q, d, sibling).wait_recv()

        for h in range(HEADS):
            lowered = (mm(qbuf[d, h], wk_ref[h]) * SCALE).astype(BF16)
            keep = lane < 64 if h % 2 == 0 else lane >= 64
            tile = qbuf[d, HEADS + h // 2].astype(F32) * SCALE
            tile = jnp.where(keep, tile, 0.0).astype(BF16)
            for part in range(2):
                tokens = slice(part * 64, (part + 1) * 64)
                qabuf[d, part, h * 64 : (h + 1) * 64, 0:RANK] = lowered[tokens]
                qabuf[d, part, h * 64 : (h + 1) * 64, RANK:KW] = tile[tokens]

        @pl.when(i == 0)
        def _():
            k_sib.wait_recv()

        s = scores(d, 0, 0)
        m = jnp.max(s, axis=1, keepdims=True)
        p = jnp.exp2(s - m)
        mbuf[d] = m
        lbuf[d] = jnp.sum(p, axis=1, keepdims=True)
        acc[d] = values(p, 0)

        @pl.when(i == 2)
        def _():
            k_up.wait_recv()
            f_up.start()
            k_down.wait_recv()
            f_down.start()

        return carry

    def far_keys(i, carry):
        d = i ^ (i // 2)
        s = scores(d, 0, 1)
        m_old = mbuf[d]
        m = jnp.maximum(m_old, jnp.max(s, axis=1, keepdims=True))
        p = jnp.exp2(s - m)
        decay = jnp.exp2(m_old - m)
        total = lbuf[d] * decay + jnp.sum(p, axis=1, keepdims=True)
        finish(d, 0, acc[d] * decay + values(p, 1), total, m)
        return carry

    def all_keys(i, carry):
        d = i ^ (i // 2)
        s0, s1 = scores(d, 1, 0), scores(d, 1, 1)
        m = jnp.maximum(
            jnp.max(s0, axis=1, keepdims=True), jnp.max(s1, axis=1, keepdims=True)
        )
        p0, p1 = jnp.exp2(s0 - m), jnp.exp2(s1 - m)
        total = jnp.sum(p0, axis=1, keepdims=True) + jnp.sum(p1, axis=1, keepdims=True)
        finish(d, 1, values(p0, 0) + values(p1, 1), total, m)
        return carry

    chips = [(0, 1), (1, 0), (3, 0), (1, 1), (3, 1), (2, 0), (2, 1)]

    def block(part, x_, zl_, k_):
        return agbuf.at[part, x_, aligned((2 * zl_ + k_) * 64, 64)]

    def merge(part):
        for j in range(4):
            i = part * 4 + j
            pltpu.make_async_copy(
                osend.at[part, 0], orecv.at[part, j], sem_o.at[1, i]
            ).wait()
            pltpu.make_async_copy(
                ssend.at[part, 0], srecv.at[part, j], sem_s.at[1, i]
            ).wait()
        lses = [srecv[part, j] for j in range(4)]
        top = jnp.maximum(
            jnp.maximum(lses[0], lses[1]), jnp.maximum(lses[2], lses[3])
        )
        shares = [jnp.exp2(lse - top) for lse in lses]
        whole = shares[0] + shares[1] + shares[2] + shares[3]
        shares = [share / whole for share in shares]
        weights = jnp.concatenate(shares + [jnp.zeros((96, 128), F32)], axis=0).T
        rows = aligned((2 * zl + k) * 64, 64)
        for h in range(HEADS):
            lanes = slice(h * VD, (h + 1) * VD)
            merged = jnp.zeros((64, VD), F32)
            for j in range(4):
                merged += weights[0:64, 8 * j + h : 8 * j + h + 1] * orecv[
                    part, j, :, lanes
                ].astype(F32)
            agbuf[part, x, rows, lanes] = merged.astype(BF16)
        here = block(part, x, zl, k)
        copies = [remote(here, here, sem_f, part * 8 + 7, sibling)]
        for i, (dx, dz) in enumerate(chips):
            device = at((x + dx) % 4, (zl + dz) % 2, k, y, zh)
            copies.append(remote(here, here, sem_ag, part * 7 + i, device))
        for copy in copies[1:] + copies[:1]:
            copy.start()
        return copies

    def pass_on(part):
        copies = []
        for i, (dx, dz) in enumerate(chips):
            there = block(part, (x + 4 - dx) % 4, (zl + dz) % 2, k)
            remote(there, there, sem_ag, part * 7 + i, sibling).wait_recv()
            copies.append(remote(there, there, sem_f, part * 8 + i, sibling))
            copies[-1].start()
        return copies

    def gathered(part):
        for i, (dx, dz) in enumerate(chips + [(0, 0)]):
            there = block(part, (x + 4 - dx) % 4, (zl + dz) % 2, 1 - k)
            remote(there, there, sem_f, part * 8 + i, sibling).wait_recv()

    own_tokens = aligned(zh * 64, 64)

    def project(part):
        total = mm_t(agbuf[part, (2 * y) % 4], wbuf[0])
        for dy in (1, 2, 3):
            total += mm_t(agbuf[part, (2 * y + dy) % 4], wbuf[dy])
        rsend[part] = total.astype(BF16)
        copies = []
        for i, d in enumerate((2, 1, 3)):
            j = (zh + d) % 4
            copies.append(
                remote(
                    rsend.at[part, aligned(j * 64, 64)],
                    rrecv.at[part, i],
                    sem_rs,
                    part * 3 + i,
                    at(x, zl, k, y, j),
                )
            )
            copies[-1].start()
        product[...] = total
        tokens = slice(part * 64, (part + 1) * 64)
        state[tokens, :] = state[tokens, :] + product[own_tokens, :]
        return copies

    lax.fori_loop(0, 4, near_keys, 0)
    f_up.wait_recv()
    f_down.wait_recv()
    sent += [f_up, f_down]
    lax.fori_loop(0, 4, far_keys, 0)
    lax.fori_loop(0, 2, all_keys, 0)
    w_copies[2].start()
    sent += merge(0)
    lax.fori_loop(2, 4, all_keys, 0)

    expert_row = jnp.broadcast_to(rt_ref[...], (TOK, TOK))
    expert = jnp.sum(jnp.where(lane == row, expert_row, 0), axis=1, keepdims=True)
    earlier = jnp.sum(
        jnp.where(jnp.logical_and(expert == expert_row, row < lane), 1, 0),
        axis=0,
        keepdims=True,
    )
    target = rt_ref[...] * CAP + earlier
    slots = lax.broadcasted_iota(jnp.int32, (2 * TOK, TOK), 0)
    select = jnp.where(slots == target, 1.0, 0.0).astype(BF16)

    for part in range(2):
        for d in range(4):

            @pl.when(jnp.logical_not(on_self(d)))
            def _():
                for copy in o_copies(d, part):
                    copy.wait_send()

    sent += pass_on(0)
    sent += merge(1)
    gathered(0)
    background.pop("w")()
    rs_copies = project(0)
    sent += pass_on(1)
    gathered(1)
    rs_copies += project(1)
    for copy in rs_copies:
        copy.wait_recv()
    sent += rs_copies
    added = []
    for part in range(2):
        rows = state[part * 64 : (part + 1) * 64, :]
        for i in range(3):
            rows += rrecv[part, i].astype(F32)
        added.append(rows)
    total = jnp.concatenate(added, axis=0)

    def three_terms(number, lanes, start):
        high = number.astype(BF16).astype(F32)
        rest = number - high
        middle = rest.astype(BF16).astype(F32)
        low = rest - middle
        return jnp.where(
            lanes == start,
            high,
            jnp.where(
                lanes == start + 1, middle, jnp.where(lanes == start + 2, low, 0.0)
            ),
        ).astype(BF16)

    squares = jnp.sum(total * total, axis=1, keepdims=True)
    pairs[:, 0:WIDTH] = (total * gain_ref[...]).astype(BF16)
    pairs[:, WIDTH:512] = three_terms(squares, lane, 64)[:, 64:128]
    dsend[...] = mm(select, pairs[...]).astype(BF16)
    experts = [(dy, dz) for dz in (2, 1, 3, 0) for dy in (2, 1, 3, 0)][:-1]
    d_copies = {}
    for i, (dy, dz) in enumerate(experts):
        peer = 4 * ((y + dy) % 4) + (zh + dz) % 4
        d_copies[dy, dz] = remote(
            dsend.at[aligned(peer * CAP, CAP)],
            drecv.at[0, 1 - dz % 2, aligned(e // 2 * CAP, CAP)],
            sem_d,
            i,
            (c, peer),
        )
        d_copies[dy, dz].start()
    drecv[0, 1, aligned(e // 2 * CAP, CAP), :] = dsend[aligned(e * CAP, CAP), :]
    d_forwards = []
    for part in range(2):
        for (dy, dz), copy in d_copies.items():
            if 1 - dz % 2 == part:
                copy.wait_recv()
        d_forwards.append(
            remote(drecv.at[0, part], drecv.at[1, part], sem_df, part, sibling)
        )
        d_forwards[-1].start()
    sent += list(d_copies.values()) + d_forwards

    background.pop("gu")()
    chip = 2 * x + zl
    own16 = aligned(chip * 16, 16)
    order = [(2, 1), (2, 0), (1, 1), (3, 1), (1, 0), (3, 0), (0, 1)]
    p_copies = []
    for part in range(2):
        d_forwards[part].wait_recv()
        rows0 = drecv[0, part, :, 0:WIDTH]
        rows1 = drecv[1, part, :, 0:WIDTH]
        for col in range(4):
            lanes = slice(col * 512, (col + 1) * 512)
            psend[part, :, lanes] = (
                mm(rows0, gubuf[0, :, lanes]) + mm(rows1, gubuf[1, :, lanes])
            ).astype(BF16)
        tail = drecv[0, part, :, 384:512].astype(F32) + drecv[
            1, part, :, 384:512
        ].astype(F32)
        squares = jnp.sum(jnp.where(lane >= 64, tail, 0.0), axis=1, keepdims=True)
        psend[part, :, FF : FF + 128] = three_terms(squares, lane, 0)
        for i, (dx, dz) in enumerate(order):
            px, pz = (x + dx) % 4, (zl + dz) % 2
            copy = remote(
                psend.at[part, aligned((2 * px + pz) * 16, 16)],
                precv.at[part, i],
                sem_p,
                part * 7 + i,
                at(px, pz, k, y, zh),
            )
            copy.start()
            p_copies.append(copy)
    sent += p_copies

    def hid_rows(side, part, dx, dz):
        source = 2 * ((x + 4 - dx) % 4) + (zl + dz) % 2
        return hid.at[side, part, aligned(source * 16, 16)]

    h_copies = []
    hf_copies = []
    for part in range(2):
        summed = psend[part, own16, :].astype(F32)
        for i in (6, 4, 5, 2, 3, 1, 0):
            p_copies[part * 7 + i].wait_recv()
            summed += precv[part, i].astype(F32)
        mean = jnp.sum(summed[:, FF : FF + 128], axis=1, keepdims=True) / D
        factor = lax.rsqrt(mean + 1e-6)
        gate = summed[:, 0:HALF] * factor
        up = summed[:, HALF:FF] * factor
        hid[0, part, own16, :] = (gate / (1.0 + jnp.exp(-gate)) * up).astype(BF16)
        here = hid.at[0, part, own16]
        for i, (dx, dz) in enumerate(chips):
            device = at((x + dx) % 4, (zl + dz) % 2, k, y, zh)
            h_copies.append(remote(here, here, sem_h, part * 7 + i, device))
            h_copies[-1].start()
        hf_copies.append(
            remote(here, hid.at[1, part, own16], sem_hf, part * 8 + 7, sibling)
        )
        hf_copies[-1].start()
    sent += h_copies
    background.pop("wd")()
    y_copies = []
    for part in range(2):
        copies = [hf_copies[part]]
        for i, (dx, dz) in enumerate(chips):
            there = hid_rows(0, part, dx, dz)
            remote(there, there, sem_h, part * 7 + i, sibling).wait_recv()
            copies.append(
                remote(
                    there, hid_rows(1, part, dx, dz), sem_hf, part * 8 + i, sibling
                )
            )
            copies[-1].start()
        down = mm_t(hid[0, part], wdbuf[:, mine])
        for copy in copies:
            copy.wait_recv()
        sent += copies
        down += mm_t(hid[1, part], wdbuf[:, other])
        ysend[part] = down.astype(BF16)

        for i, (dy, dz) in enumerate(experts):
            if 1 - dz % 2 == part:
                peer = 4 * ((y + dy) % 4) + (zh + dz) % 4
                copy = remote(
                    ysend.at[part, aligned(peer // 2 * CAP, CAP)],
                    yrecv.at[aligned(e * CAP, CAP)],
                    sem_y,
                    i,
                    (c, peer),
                )
                copy.start()
                y_copies.append(copy)
    yrecv[aligned(e * CAP, CAP), :] = ysend[1, aligned(e // 2 * CAP, CAP), :]
    for copy in y_copies:
        copy.wait_recv()
    sent += y_copies
    routed = lax.dot_general(
        yrecv[...], select, (((0,), (0,)), ((), ())), preferred_element_type=F32
    )
    out_ref[...] = (total.T + routed * rw_ref[...]).astype(BF16)

    for copy in sent:
        copy.wait_send()


def per_device(
    queries,
    latent_cache,
    group_latent,
    w_absorb_k,
    value_absorb_weight,
    w_out,
    residual,
    norm_gain,
    routes,
    route_weight,
    w_gate,
    w_up,
    w_down,
):
    vmem = pl.BlockSpec(memory_space=pltpu.VMEM)
    hbm = pl.BlockSpec(memory_space=pl.ANY)
    dma = pltpu.SemaphoreType.DMA
    return pl.pallas_call(
        kernel,
        out_shape=jax.ShapeDtypeStruct((WIDTH, TOK), BF16),
        in_specs=[vmem] * 5 + [hbm] + [vmem] * 4 + [hbm] * 3,
        out_specs=vmem,
        scratch_shapes=[
            pltpu.VMEM((4, 6, TOK, 128), BF16),
            pltpu.VMEM((2, KW, 2 * KEYS), BF16),
            pltpu.VMEM((4, 2, HEADS * 64, KW), BF16),
            pltpu.VMEM((4, HEADS * 64, RANK), F32),
            pltpu.VMEM((4, HEADS * 64, 1), F32),
            pltpu.VMEM((4, HEADS * 64, 1), F32),
            pltpu.VMEM((2, 4, 64, HEADS * VD), BF16),
            pltpu.VMEM((2, 4, 8, 128), F32),
            pltpu.VMEM((2, 4, 64, HEADS * VD), BF16),
            pltpu.VMEM((2, 4, 8, 128), F32),
            pltpu.VMEM((2, 4, 4 * 64, HEADS * VD), BF16),
            pltpu.VMEM((4, WIDTH, HEADS * VD), BF16),
            pltpu.VMEM((4 * 64, WIDTH), F32),
            pltpu.VMEM((2, 4 * 64, WIDTH), BF16),
            pltpu.VMEM((2, 3, 64, WIDTH), BF16),
            pltpu.VMEM((TOK, WIDTH), F32),
            pltpu.VMEM((TOK, 512), BF16),
            pltpu.VMEM((2 * TOK, 512), BF16),
            pltpu.VMEM((2, 2, TOK, 512), BF16),
            pltpu.VMEM((2, WIDTH, FF), BF16),
            pltpu.VMEM((WIDTH, FF), BF16),
            pltpu.VMEM((2, TOK, FF + 128), BF16),
            pltpu.VMEM((2, 7, 16, FF + 128), BF16),
            pltpu.VMEM((2, 2, TOK, HALF), BF16),
            pltpu.VMEM((2, TOK, WIDTH), BF16),
            pltpu.VMEM((2 * TOK, WIDTH), BF16),
            dma((2, 4)),
            dma((2, 5)),
            dma((2, 4)),
            dma((2, 4)),
            dma,
            dma((2, 8)),
            dma((2, 8)),
            dma((2, 14)),
            dma((2, 16)),
            dma((2, 6)),
            dma((2, 15)),
            dma((2, 2)),
            dma((2, 14)),
            dma((2, 14)),
            dma((2, 16)),
            dma((2, 15)),
        ],
        compiler_params=pltpu.CompilerParams(
            collective_id=0, has_side_effects=True, vmem_limit_bytes=56 * 2**20
        ),
        name="layer",
    )(
        queries.transpose(1, 2, 0),
        latent_cache.T,
        group_latent.T,
        w_absorb_k,
        value_absorb_weight,
        w_out.T,
        residual.T,
        norm_gain.reshape(1, WIDTH),
        routes.T,
        route_weight.T,
        w_gate,
        w_up,
        w_down.transpose(0, 2, 1),
    ).T


def solution(mesh):
    in_specs = (
        P("ctx", "exp", None),
        P("ctx", None),
        P("ctx", None),
        P("exp", None, None),
        P("exp", None, None),
        P("exp", "ctx"),
        P("exp", "ctx"),
        P("ctx"),
        P("exp", None),
        P("exp", None),
        P("exp", "ctx", None),
        P("exp", "ctx", None),
        P("exp", None, "ctx"),
    )
    out_specs = P("exp", "ctx")
    return jax.shard_map(
        per_device, mesh=mesh, in_specs=in_specs, out_specs=out_specs, check_vma=False
    )
```

time: 458 us -> 124 us (0.27)
  waiting for transfers between devices: 339 us -> 0 us
  Pallas kernels: 0 us -> 123 us
  blocking collectives: 63.8 us -> 0 us
  matrix products: 26.9 us -> 0 us
  between operations: 13.4 us -> 0.01 us
  other arithmetic: 7.17 us -> 0 us
  local copies, waits for them, and re-layouts: 7.3 us -> 1.55 us
    all_gather x3 -> x0, waiting for transfers between devices: 128 us -> none  [the longest x1 47.3 us: per_device(): lax.all_gather(latent_cache, 'ctx', axis=0, tiled=True)]
    psum x1 -> x0, waiting for transfers between devices: 123 us -> none  [per_device(): summed = lax.psum(stacked.astype(jnp.bfloat16), 'ctx').astype(jnp.float32)]
    pallas_call x0 -> x1, Pallas kernels: none -> 123 us  [per_device(): pl.pallas_call(kernel, out_shape=jax.ShapeDtypeStruct((WIDTH, TOK), BF16)...]
    unnamed x6 -> x0, waiting for transfers between devices: 87.5 us -> none
    all_to_all x2 -> x0, blocking collectives: 34.8 us -> none  [the longest x1 19.2 us: per_device(): lax.all_to_all(expert_out.reshape(sources, slots, width), 'exp', split_ax...]
    psum x1 -> x0, blocking collectives: 29 us -> none  [per_device(): square_sums = lax.psum(jnp.sum(state * state, axis=1), 'ctx')]
    dot_general x12 -> x0, matrix products: 26.9 us -> none  [the longest x2 11.4 us: fold_keys(): lax.dot_general(absorbed_query, piece, (((1,), (1,)), ((), ())), preferre...]
  transfers between devices with their start and end apart: 5 -> 0, of which waited for: 5 -> 0; matrix products, arithmetic and copies ran while one was open for 2% -> 0% of each run, Pallas kernels for 0% -> 0%
where the time goes in v2:
time: 124 us
  Pallas kernels  123 us (99%)
  local copies, waits for them, and re-layouts  1.55 us (1%)
    pallas_call x1, Pallas kernels, per_device(): pl.pallas_call(kernel, out_shape=jax.ShapeDtypeStruct((WIDTH, TOK), BF16)...  123 us

profile of v2, /device:TPU:1, one launch (start us, length us, event | category | flops | bytes accessed | tf_op | source)
XLA Modules:
  0.0 124.4 jit_solution(6362156460272020822)
XLA Ops:
  0.0 122.8 %layer.1 = bf16[448,128]{1,0:T(8,128)(2,1)} custom-call(bf16[4,192,128]{2,1,0:T(8,128)(2,1)} %bitcast.14, bf16[576,256]{1,0:T(8,128)(2,1)} %bitcast.13, bf16[576,128]{1,0:T(8,128)(2,1)} %bitcast.15, bf16[4,128,512]{2,1,0:T(8,128)(2,1)} %wk_ref.1, bf16[4,512,128]{2,1,0:T(8,128)(2,1)} %wv_ref.1, bf16[448,512]{1,0:T(8,128)(2,1)} %bitcast.12, ...), custom_call_target="tpu_custom_call" | custom-call | tf_op jit(solution)/shard_map/layer/pallas_call | solution.py:634
  122.8 1.6 %copy.15 = bf16[128,448]{0,1:T(8,128)(2,1)} copy(bf16[128,448]{0,1:T(8,128)(2,1)} %bitcast.11) | data formatting | bytes 229376

commit v3 on v2

--- a/solution.py
+++ b/solution.py
@@ -198,8 +198,6 @@
             )
         )
     wd_copy = pltpu.make_async_copy(wd_ref.at[0], wdbuf, sem_wd)
-    for copy in gu_local + gu_remote + [wd_copy]:
-        copy.start()
 
     def w_ready():
         for copy in w_copies:
@@ -421,15 +419,19 @@
         state[tokens, :] = state[tokens, :] + product[own_tokens, :]
         return copies
 
-    lax.fori_loop(0, 4, near_keys, 0)
+    lax.fori_loop(0, 3, near_keys, 0)
     f_up.wait_recv()
     f_down.wait_recv()
     sent += [f_up, f_down]
-    lax.fori_loop(0, 4, far_keys, 0)
-    lax.fori_loop(0, 2, all_keys, 0)
+    lax.fori_loop(0, 3, far_keys, 0)
+    lax.fori_loop(3, 4, near_keys, 0)
+    lax.fori_loop(3, 4, far_keys, 0)
+    for copy in gu_local + gu_remote + [wd_copy]:
+        copy.start()
+    lax.fori_loop(0, 3, all_keys, 0)
+    sent += merge(0)
+    lax.fori_loop(3, 4, all_keys, 0)
     w_copies[2].start()
-    sent += merge(0)
-    lax.fori_loop(2, 4, all_keys, 0)
 
     expert_row = jnp.broadcast_to(rt_ref[...], (TOK, TOK))
     expert = jnp.sum(jnp.where(lane == row, expert_row, 0), axis=1, keepdims=True)
@@ -442,16 +444,8 @@
     slots = lax.broadcasted_iota(jnp.int32, (2 * TOK, TOK), 0)
     select = jnp.where(slots == target, 1.0, 0.0).astype(BF16)
 
-    for part in range(2):
-        for d in range(4):
-
-            @pl.when(jnp.logical_not(on_self(d)))
-            def _():
-                for copy in o_copies(d, part):
-                    copy.wait_send()
-
+    sent += merge(1)
     sent += pass_on(0)
-    sent += merge(1)
     gathered(0)
     background.pop("w")()
     rs_copies = project(0)
@@ -486,7 +480,7 @@
     pairs[:, 0:WIDTH] = (total * gain_ref[...]).astype(BF16)
     pairs[:, WIDTH:512] = three_terms(squares, lane, 64)[:, 64:128]
     dsend[...] = mm(select, pairs[...]).astype(BF16)
-    experts = [(dy, dz) for dz in (2, 1, 3, 0) for dy in (2, 1, 3, 0)][:-1]
+    experts = [(dy, dz) for dz in (1, 3, 2, 0) for dy in (2, 1, 3, 0)][:-1]
     d_copies = {}
     for i, (dy, dz) in enumerate(experts):
         peer = 4 * ((y + dy) % 4) + (zh + dz) % 4
@@ -609,6 +603,13 @@
     )
     out_ref[...] = (total.T + routed * rw_ref[...]).astype(BF16)
 
+    for part in range(2):
+        for d in range(4):
+
+            @pl.when(jnp.logical_not(on_self(d)))
+            def _():
+                for copy in o_copies(d, part):
+                    copy.wait_send()
     for copy in sent:
         copy.wait_send()
 

time: 124 us -> 116 us (0.935)
  Pallas kernels: 123 us -> 114 us
    pallas_call x1, Pallas kernels: 123 us -> 114 us  [per_device(): pl.pallas_call(kernel, out_shape=jax.ShapeDtypeStruct((WIDTH, TOK), BF16)...]
where the time goes in v3:
time: 116 us
  Pallas kernels  114 us (98%)
  local copies, waits for them, and re-layouts  1.55 us (1%)
    pallas_call x1, Pallas kernels, per_device(): pl.pallas_call(kernel, out_shape=jax.ShapeDtypeStruct((WIDTH, TOK), BF16)...  114 us

profile of v3, /device:TPU:1, one launch (start us, length us, event | category | flops | bytes accessed | tf_op | source)
XLA Modules:
  0.0 115.8 jit_solution(6195294900978197983)
XLA Ops:
  0.0 114.2 %layer.1 = bf16[448,128]{1,0:T(8,128)(2,1)} custom-call(bf16[4,192,128]{2,1,0:T(8,128)(2,1)} %bitcast.14, bf16[576,256]{1,0:T(8,128)(2,1)} %bitcast.13, bf16[576,128]{1,0:T(8,128)(2,1)} %bitcast.15, bf16[4,128,512]{2,1,0:T(8,128)(2,1)} %wk_ref.1, bf16[4,512,128]{2,1,0:T(8,128)(2,1)} %wv_ref.1, bf16[448,512]{1,0:T(8,128)(2,1)} %bitcast.12, ...), custom_call_target="tpu_custom_call" | custom-call | tf_op jit(solution)/shard_map/layer/pallas_call | solution.py:635
  114.2 1.6 %copy.15 = bf16[128,448]{0,1:T(8,128)(2,1)} copy(bf16[128,448]{0,1:T(8,128)(2,1)} %bitcast.11) | data formatting | bytes 229376

commit v4 on v3

--- a/solution.py
+++ b/solution.py
@@ -423,14 +423,14 @@
     f_up.wait_recv()
     f_down.wait_recv()
     sent += [f_up, f_down]
-    lax.fori_loop(0, 3, far_keys, 0)
+    lax.fori_loop(0, 3, far_keys, 0, unroll=3)
     lax.fori_loop(3, 4, near_keys, 0)
     lax.fori_loop(3, 4, far_keys, 0)
     for copy in gu_local + gu_remote + [wd_copy]:
         copy.start()
-    lax.fori_loop(0, 3, all_keys, 0)
+    lax.fori_loop(0, 2, all_keys, 0, unroll=2)
     sent += merge(0)
-    lax.fori_loop(3, 4, all_keys, 0)
+    lax.fori_loop(2, 4, all_keys, 0, unroll=2)
     w_copies[2].start()
 
     expert_row = jnp.broadcast_to(rt_ref[...], (TOK, TOK))
@@ -508,32 +508,35 @@
     chip = 2 * x + zl
     own16 = aligned(chip * 16, 16)
     order = [(2, 1), (2, 0), (1, 1), (3, 1), (1, 0), (3, 0), (0, 1)]
+    widths = (slice(0, HALF + 128), slice(0, HALF))
     p_copies = []
     for part in range(2):
         d_forwards[part].wait_recv()
         rows0 = drecv[0, part, :, 0:WIDTH]
         rows1 = drecv[1, part, :, 0:WIDTH]
-        for col in range(4):
-            lanes = slice(col * 512, (col + 1) * 512)
-            psend[part, :, lanes] = (
-                mm(rows0, gubuf[0, :, lanes]) + mm(rows1, gubuf[1, :, lanes])
-            ).astype(BF16)
         tail = drecv[0, part, :, 384:512].astype(F32) + drecv[
             1, part, :, 384:512
         ].astype(F32)
         squares = jnp.sum(jnp.where(lane >= 64, tail, 0.0), axis=1, keepdims=True)
-        psend[part, :, FF : FF + 128] = three_terms(squares, lane, 0)
-        for i, (dx, dz) in enumerate(order):
-            px, pz = (x + dx) % 4, (zl + dz) % 2
-            copy = remote(
-                psend.at[part, aligned((2 * px + pz) * 16, 16)],
-                precv.at[part, i],
-                sem_p,
-                part * 7 + i,
-                at(px, pz, k, y, zh),
-            )
-            copy.start()
-            p_copies.append(copy)
+        psend[part, 0, :, HALF : HALF + 128] = three_terms(squares, lane, 0)
+        for col in range(2):
+            for side in range(2):
+                lanes = slice(side * HALF + col * 512, side * HALF + (col + 1) * 512)
+                psend[part, col, :, side * 512 : (side + 1) * 512] = (
+                    mm(rows0, gubuf[0, :, lanes]) + mm(rows1, gubuf[1, :, lanes])
+                ).astype(BF16)
+            for i, (dx, dz) in enumerate(order):
+                px, pz = (x + dx) % 4, (zl + dz) % 2
+                rows = aligned((2 * px + pz) * 16, 16)
+                copy = remote(
+                    psend.at[part, col, rows, widths[col]],
+                    precv.at[part, col, i, :, widths[col]],
+                    sem_p,
+                    (part * 2 + col) * 7 + i,
+                    at(px, pz, k, y, zh),
+                )
+                copy.start()
+                p_copies.append(copy)
     sent += p_copies
 
     def hid_rows(side, part, dx, dz):
@@ -543,22 +546,34 @@
     h_copies = []
     hf_copies = []
     for part in range(2):
-        summed = psend[part, own16, :].astype(F32)
-        for i in (6, 4, 5, 2, 3, 1, 0):
-            p_copies[part * 7 + i].wait_recv()
-            summed += precv[part, i].astype(F32)
-        mean = jnp.sum(summed[:, FF : FF + 128], axis=1, keepdims=True) / D
-        factor = lax.rsqrt(mean + 1e-6)
-        gate = summed[:, 0:HALF] * factor
-        up = summed[:, HALF:FF] * factor
-        hid[0, part, own16, :] = (gate / (1.0 + jnp.exp(-gate)) * up).astype(BF16)
-        here = hid.at[0, part, own16]
-        for i, (dx, dz) in enumerate(chips):
-            device = at((x + dx) % 4, (zl + dz) % 2, k, y, zh)
-            h_copies.append(remote(here, here, sem_h, part * 7 + i, device))
-            h_copies[-1].start()
+        for col in range(2):
+            summed = psend[part, col, own16, widths[col]].astype(F32)
+            for i in (6, 4, 5, 2, 3, 1, 0):
+                p_copies[(part * 2 + col) * 7 + i].wait_recv()
+                summed += precv[part, col, i, :, widths[col]].astype(F32)
+            if col == 0:
+                mean = jnp.sum(summed[:, HALF:], axis=1, keepdims=True) / D
+                factor = lax.rsqrt(mean + 1e-6)
+            gate = summed[:, 0:512] * factor
+            up = summed[:, 512:HALF] * factor
+            lanes = slice(col * 512, (col + 1) * 512)
+            hid[0, part, own16, lanes] = (
+                gate / (1.0 + jnp.exp(-gate)) * up
+            ).astype(BF16)
+            here = hid.at[0, part, own16, lanes]
+            for i, (dx, dz) in enumerate(chips):
+                device = at((x + dx) % 4, (zl + dz) % 2, k, y, zh)
+                i += (part * 2 + col) * 7
+                h_copies.append(remote(here, here, sem_h, i, device))
+                h_copies[-1].start()
         hf_copies.append(
-            remote(here, hid.at[1, part, own16], sem_hf, part * 8 + 7, sibling)
+            remote(
+                hid.at[0, part, own16],
+                hid.at[1, part, own16],
+                sem_hf,
+                part * 8 + 7,
+                sibling,
+            )
         )
         hf_copies[-1].start()
     sent += h_copies
@@ -568,7 +583,11 @@
         copies = [hf_copies[part]]
         for i, (dx, dz) in enumerate(chips):
             there = hid_rows(0, part, dx, dz)
-            remote(there, there, sem_h, part * 7 + i, sibling).wait_recv()
+            for col in range(2):
+                piece = there.at[:, col * 512 : (col + 1) * 512]
+                remote(
+                    piece, piece, sem_h, (part * 2 + col) * 7 + i, sibling
+                ).wait_recv()
             copies.append(
                 remote(
                     there, hid_rows(1, part, dx, dz), sem_hf, part * 8 + i, sibling
@@ -659,8 +678,8 @@
             pltpu.VMEM((2, 2, TOK, 512), BF16),
             pltpu.VMEM((2, WIDTH, FF), BF16),
             pltpu.VMEM((WIDTH, FF), BF16),
-            pltpu.VMEM((2, TOK, FF + 128), BF16),
-            pltpu.VMEM((2, 7, 16, FF + 128), BF16),
+            pltpu.VMEM((2, 2, TOK, HALF + 128), BF16),
+            pltpu.VMEM((2, 2, 7, 16, HALF + 128), BF16),
             pltpu.VMEM((2, 2, TOK, HALF), BF16),
             pltpu.VMEM((2, TOK, WIDTH), BF16),
             pltpu.VMEM((2 * TOK, WIDTH), BF16),
@@ -676,8 +695,8 @@
             dma((2, 6)),
             dma((2, 15)),
             dma((2, 2)),
-            dma((2, 14)),
-            dma((2, 14)),
+            dma((2, 28)),
+            dma((2, 28)),
             dma((2, 16)),
             dma((2, 15)),
         ],

time: 116 us -> 115 us (level)
  no operation moved by 1% of the time
where the time goes in v4:
time: 115 us
  Pallas kernels  113 us (98%)
  local copies, waits for them, and re-layouts  1.55 us (1%)
    pallas_call x1, Pallas kernels, per_device(): pl.pallas_call(kernel, out_shape=jax.ShapeDtypeStruct((WIDTH, TOK), BF16)...  113 us

profile of v4, /device:TPU:1, one launch (start us, length us, event | category | flops | bytes accessed | tf_op | source)
XLA Modules:
  0.0 114.8 jit_solution(12957628617607184143)
XLA Ops:
  0.0 113.2 %layer.1 = bf16[448,128]{1,0:T(8,128)(2,1)} custom-call(bf16[4,192,128]{2,1,0:T(8,128)(2,1)} %bitcast.14, bf16[576,256]{1,0:T(8,128)(2,1)} %bitcast.13, bf16[576,128]{1,0:T(8,128)(2,1)} %bitcast.15, bf16[4,128,512]{2,1,0:T(8,128)(2,1)} %wk_ref.1, bf16[4,512,128]{2,1,0:T(8,128)(2,1)} %wv_ref.1, bf16[448,512]{1,0:T(8,128)(2,1)} %bitcast.12, ...), custom_call_target="tpu_custom_call" | custom-call | tf_op jit(solution)/shard_map/layer/pallas_call | solution.py:654
  113.2 1.6 %copy.15 = bf16[128,448]{0,1:T(8,128)(2,1)} copy(bf16[128,448]{0,1:T(8,128)(2,1)} %bitcast.11) | data formatting | bytes 229376
